TPU v7x, 128 devices: a whole 4x4x4 slice. The times are simulated.
128 devices in a mesh: group: 4 (over z_lo, core), cells: 32 (over y, x, z_hi).
Axes of the slice: x: 4, y: 4, z: 4 (z_hi: 2, z_lo: 2; z = z_hi * 2 + z_lo), core: 2. Of those that a mesh axis runs over, the one named last changes fastest.
Arguments:
- state: float32 [4, 3, 90, 131072], P('group', None, None, 'cells'), may hold values from -6 to 6
- vertical_mix: float32 [4, 90, 131072], P('group', None, 'cells'), may hold values from 0.02 to 0.2
- neighbour_weight: float32 [4, 3, 131072], P('group', None, 'cells'), may hold values from 0.02 to 0.15
- neighbours: int32 [4, 3, 131072], P('group', None, 'cells'), may hold values from 0 to 4607, as said below
- land_sea: int32 [131072], P('cells'), may hold values 0 or 1
- remap_weight: float32 [4, 2, 8192, 256], P('group', None, 'cells'), may hold values from 0 to 0.25, as said below
- pair_offsets: int32 [4, 32, 4], P('group', 'cells'), may hold values from 0 to 3840, as said below
- pair_rows: int32 [4, 32, 2], P('group', 'cells'), may hold values from 128 to 256
Outputs:
- new_state: float32 [4, 3, 90, 131072], P('group', None, None, 'cells')
Inputs may be any that keep to these rules, and one draw needn't show every extreme that they name: Neighbour positions lie within one rim of the cell; the first two neighbours lie within 4 cells of the cell; both outermost rim cells are used by some cell of every device. `remap_weight`: remap weights are zero where the row and column within a block differ by 4 or more. `pair_offsets`: offsets keep every block inside its device's cells; the ocean rows of strip g's blocks lie in [g * 1365, (g + 1) * 1365).
All inputs are finite; a program needn't handle non-finite values. No bound on the sum of `land_sea` on one device may be relied on, other than what follows from the above.
Results may differ from a plain program's by a relative error of at most 0.0003.
Values sent between devices are 32-bit elements; how exact they have to be, the bound alone decides.
A program may use at most 128 MiB of HBM per device.

v0:
```python
import jax
import jax.numpy as jnp
from jax import lax
from jax.sharding import PartitionSpec as P

SEGMENTS = 2
HALO = 256


near_reach = 4


def from_root(value, axis, source):
    kept = jnp.where(lax.axis_index(axis) == source, value, 0).astype(value.dtype)
    return lax.psum(kept, axis)


def passed_along(block, axis, distance):
    devices = range(lax.axis_size(axis))
    route = [((i - distance) % len(devices), i) for i in devices]
    return lax.ppermute(block, axis, route)


def with_halo(cells, sides, width):
    for axis, dim in sides:
        count = lax.axis_size(axis)
        head = lax.slice_in_dim(cells, 0, width, axis=dim)
        tail = lax.slice_in_dim(cells, cells.shape[dim] - width, cells.shape[dim], axis=dim)
        cells = jnp.concatenate(
            [
                lax.ppermute(tail, axis, [(i, (i + 1) % count) for i in range(count)]),
                cells,
                lax.ppermute(head, axis, [((i + 1) % count, i) for i in range(count)]),
            ],
            axis=dim,
        )
    return cells


def pair_coupling(near_air, sea_here, sea_left, weights, offsets, rows, keep):
    pair_height = weights.shape[1]
    pair_width = weights.shape[2]
    columns = near_air.shape[1]
    air_gap = jnp.zeros((2, columns), jnp.float32)
    sea_pair = (sea_here, sea_left)
    blocks = []
    for which in range(2):
        col_start = offsets[2 * which]
        row_start = offsets[2 * which + 1]
        live_rows = (jnp.arange(pair_height, dtype=jnp.int32) < rows[which]).astype(jnp.float32)
        block_weight = weights[which] * live_rows[:, None]
        sea_rows = lax.dynamic_slice(sea_pair[which], (jnp.int32(0), row_start), (3, pair_height))
        air_rows = lax.dynamic_slice(near_air, (jnp.int32(0), col_start), (2, pair_width))
        contrib = jnp.dot(sea_rows[:2], block_weight, precision=lax.Precision.HIGHEST)
        contrib = contrib - air_rows * jnp.dot(
            sea_rows[2:3], block_weight, precision=lax.Precision.HIGHEST
        )
        window = lax.dynamic_slice(air_gap, (jnp.int32(0), col_start), (2, pair_width))
        air_gap = lax.dynamic_update_slice(air_gap, window + contrib, (jnp.int32(0), col_start))
        blocks.append((block_weight, col_start, row_start))
    air_flux = 0.5 * air_gap * keep
    ocean_terms = []
    for block_weight, col_start, row_start in blocks:
        flux_rows = lax.dynamic_slice(air_flux, (jnp.int32(0), col_start), (2, pair_width))
        ocean_part = jnp.dot(flux_rows, block_weight.T, precision=lax.Precision.HIGHEST)
        ocean_terms.append(
            lax.dynamic_update_slice(
                jnp.zeros((2, columns), jnp.float32), ocean_part, (jnp.int32(0), row_start)
            )
        )
    return (air_flux, ocean_terms)


def vertical_term(fields, mixing):
    upward = (fields[:, 1:] - fields[:, :-1]) * mixing[None, :-1]
    zero_row = jnp.zeros_like(fields[:, :1])
    return jnp.concatenate([upward, zero_row], 1) - jnp.concatenate([zero_row, upward], 1)


def neighbour_mix(source, positions, weights, width):
    centre = jnp.arange(width, dtype=jnp.int32)[None, :] + HALO
    offsets = positions[:2] - centre
    mixed = weights[2][None, None, :] * jnp.take(source, positions[2], axis=2)
    for step in range(-near_reach, near_reach + 1):
        coeff = jnp.where(offsets[0] == step, weights[0], 0.0) + jnp.where(
            offsets[1] == step, weights[1], 0.0
        )
        moved = lax.slice_in_dim(source, HALO + step, HALO + step + width, axis=2)
        mixed = mixed + coeff[None, None, :] * moved
    return mixed


def per_device(
    state,
    vertical_mix,
    neighbour_weight,
    neighbours,
    land_sea,
    remap_weight,
    pair_offsets,
    pair_rows,
):
    groups = lax.axis_size("group")
    is_ocean = lax.axis_index("group") == groups - 1
    keep_air = jnp.where(is_ocean, 0.0, 1.0).astype(jnp.float32)
    sea_mask = land_sea.astype(jnp.float32)
    scale_row = jnp.where(is_ocean, sea_mask, jnp.ones_like(sea_mask))
    scale = scale_row[None, None, :]
    fields = state[0]
    near_air = fields[:2, 0, :]
    mixing = vertical_mix[0]
    weight_set = neighbour_weight[0]
    places = neighbours[0]
    columns = fields.shape[2]
    weight_total = weight_set[0] + weight_set[1] + weight_set[2]
    current = fields
    sea_values = jnp.concatenate([near_air * sea_mask[None], sea_mask[None]], 0)
    sea_here = from_root(sea_values, "group", groups - 1)
    sea_left = passed_along(sea_here, "cells", 1)
    air_flux, ocean_terms = pair_coupling(
        near_air, sea_here, sea_left, remap_weight[0], pair_offsets[0, 0], pair_rows[0, 0], keep_air
    )
    moved = passed_along(ocean_terms[1], "cells", -1)
    ocean_flux = lax.psum(ocean_terms[0] + moved, "group")
    forcing = jnp.where(is_ocean, -ocean_flux * sea_mask[None], air_flux)
    for segment in range(SEGMENTS):
        padded = with_halo(current, (("cells", 2),), HALO)
        gathered = neighbour_mix(padded, places, weight_set, columns)
        horizontal = gathered - weight_total[None, None, :] * current
        current = current + (horizontal + vertical_term(current, mixing)) * scale
    current = current.at[:2, 0, :].add(forcing)
    return current[None]


def solution(mesh):
    return jax.shard_map(
        per_device,
        mesh=mesh,
        in_specs=(
            P("group", None, None, "cells"),
            P("group", None, "cells"),
            P("group", None, "cells"),
            P("group", None, "cells"),
            P("cells"),
            P("group", None, "cells", None),
            P("group", "cells", None),
            P("group", "cells", None),
        ),
        out_specs=P("group", None, None, "cells"),
        check_vma=False,
    )
```

profile of v0, /device:TPU:1, one launch (start us, length us, event | category | flops | bytes accessed | tf_op | source)
XLA Modules:
  0.0 322.3 jit_solution(14457559293984095424)
XLA Ops:
  0.1 9.1 %copy.22 = f32[1,3,90,4096]{3,1,2,0:T(4,128)} copy(f32[1,3,90,4096]{3,0,2,1:T(1,128)} %param.12) | data formatting | bytes 8847360 | tf_op args[0]
  10.1 12.6 %psum.14 = f32[3,4096]{1,0:T(4,128)} all-reduce(f32[3,4096]{1,0:T(4,128)S(1)} %maximum_select_fusion), channel_id=1, replica_groups=mesh['group'=4,'cells'=32] {'group'}, use_global_device_ids=true, to_apply=%region_0.2 | all-reduce | flops 12288 | bytes 98304 | tf_op jit(solution)/shard_map/psum | solution.py:15
  22.6 3.3 %collective-permute-start.4 = (f32[3,4096]{1,0:T(4,128)}, f32[3,4096]{1,0:T(4,128)}, u32[]{:S(2)}, u32[]{:S(2)}) collective-permute-start(f32[3,4096]{1,0:T(4,128)} %psum.14), channel_id=1, source_target_pairs={{31,0},{0,1},{1,2},{2,3},{3,4},{4,5},{5,6},{6,7},{7,8},{8,9},{9,10... | collective-permute-start | bytes 147464 | tf_op jit(solution)/shard_map/ppermute | solution.py:21
  26.0 2.1 fusion.95
  28.6 6.6 %collective-permute-start.1 = (f32[3,90,256]{2,0,1:T(4,128)}, f32[3,90,256]{2,0,1:T(4,128)}, u32[]{:S(2)}, u32[]{:S(2)}) collective-permute-start(f32[3,90,256]{2,0,1:T(4,128)} %get-tuple-element.21), channel_id=1, source_target_pairs={{1,0},{2,1},{3,2},{4,3},{5,4},{6,5},{7,6},{8,7},{9,8},{10,9},{11,1... | collective-permute-start | bytes 829448 | tf_op jit(solution)/shard_map/ppermute | solution.py:33
  45.2 4.3 %fusion.55 = f32[3,89,4096]{2,0,1:T(4,128)} fusion(f32[3,90,4096]{2,0,1:T(4,128)S(1)} %bitcast.159, f32[89,4096]{1,0:T(8,128)S(1)} %bitcast.161), kind=kLoop, calls=%fused_computation.84 | loop fusion | flops 2187264 | bytes 14581760 | tf_op jit(solution)/shard_map/mul | solution.py:75
  61.1 3.8 %collective-permute-done.5 = f32[2,4096]{1,0:T(2,128)S(1)} collective-permute-done((f32[2,4096]{1,0:T(2,128)S(1)}, f32[2,4096]{1,0:T(2,128)S(1)}, u32[]{:S(2)}, u32[]{:S(2)}) %collective-permute-start.5) | collective-permute-done | bytes 32800 | tf_op jit(solution)/shard_map/ppermute | solution.py:21
  65.6 13.1 %psum.15 = f32[2,4096]{1,0:T(2,128)S(1)} all-reduce(f32[2,4096]{1,0:T(2,128)S(1)} %add.218), channel_id=1, replica_groups=mesh['group'=4,'cells'=32] {'group'}, use_global_device_ids=true, to_apply=%region_1.3 | all-reduce | flops 8192 | bytes 65536 | tf_op jit(solution)/shard_map/psum | solution.py:124
  78.7 7.1 %pad_maximum_fusion = f32[3,90,4608]{2,0,1:T(4,128)} fusion(f32[3,90,256]{2,0,1:T(4,128)} %collective-permute-done.1, f32[3,90,4096]{2,0,1:T(4,128)} %bitcast.157, f32[3,90,256]{2,0,1:T(4,128)S(1)} %collective-permute-done), kind=kLoop, calls=%fused_computation.14 | loop fusion | flops 2488320 | bytes 9953280 | tf_op jit(solution)/shard_map/concatenate | solution.py:29
  85.8 11.3 %copy.12 = f32[3,90,4608]{1,0,2:T(4,128)} copy(f32[3,90,4608]{2,0,1:T(4,128)} %pad_maximum_fusion) | data formatting | bytes 9953280 | tf_op jit(solution)/shard_map/concatenate | solution.py:29
  97.1 33.7 %gather_fusion = f32[4096,3,90]{2,1,0:T(4,128)} fusion(f32[3,90,4608]{1,0,2:T(4,128)} %copy.12, s32[4096]{0:T(1024)S(1)} %fusion.88), kind=kCustom, calls=%fused_computation.clone | custom fusion | bytes 8863744 | tf_op jit(solution)/shard_map/jit(_take)/gather | solution.py:83
  130.8 10.7 %copy.13 = f32[4096,3,90]{0,1,2:T(4,128)} copy(f32[4096,3,90]{2,1,0:T(4,128)} %gather_fusion) | data formatting | bytes 8847360 | tf_op jit(solution)/shard_map/jit(_take)/gather | solution.py:83
  141.6 46.0 %fusion.32 = f32[3,90,4096]{2,0,1:T(4,128)S(1)} fusion(f32[3,90,4096]{2,0,1:T(4,128)} %bitcast.158, f32[3,90,256]{2,0,1:T(4,128)} %collective-permute-done.1, f32[3,90,256]{2,0,1:T(4,128)S(1)} %collective-permute-done, f32[4096,3,90]{0,1,2:T(4,128)} %copy.13, f32[3,89,4096]{2,0,1:T(4,128)} %fusion.55, f32[4096]{0:T(1024)S(1)} %broadcast_select_fusion, ...), kind=kLoop, calls=%fused_computation.48 | loop fusion | flops 37601280 | bytes 18399232 | tf_op jit(solution)/shard_map/add | solution.py:130
  187.8 7.2 %collective-permute-start.3 = (f32[3,90,256]{2,0,1:T(4,128)S(1)}, f32[3,90,256]{2,0,1:T(4,128)S(1)}, u32[]{:S(2)}, u32[]{:S(2)}) collective-permute-start(f32[3,90,256]{2,0,1:T(4,128)S(1)} %get-tuple-element.19), channel_id=1, source_target_pairs={{1,0},{2,1},{3,2},{4,3},{5,4},{6,5},{7,6},{8,7},{9,8},{10,9},{11,1... | collective-permute-start | bytes 829448 | tf_op jit(solution)/shard_map/ppermute | solution.py:33
  195.0 4.3 %fusion.54 = f32[3,89,4096]{2,0,1:T(4,128)} fusion(f32[3,90,4096]{2,0,1:T(4,128)S(1)} %fusion.32, f32[89,4096]{1,0:T(8,128)S(1)} %bitcast.162), kind=kLoop, calls=%fused_computation.82 | loop fusion | flops 2187264 | bytes 14581760 | tf_op jit(solution)/shard_map/mul | solution.py:75
  199.2 3.6 %collective-permute-done.2 = f32[3,90,256]{2,0,1:T(4,128)S(1)} collective-permute-done((f32[3,90,256]{2,0,1:T(4,128)S(1)}, f32[3,90,256]{2,0,1:T(4,128)S(1)}, u32[]{:S(2)}, u32[]{:S(2)}) %collective-permute-start.2) | collective-permute-done | bytes 276512 | tf_op jit(solution)/shard_map/ppermute | solution.py:31
  202.9 3.7 %collective-permute-done.3 = f32[3,90,256]{2,0,1:T(4,128)S(1)} collective-permute-done((f32[3,90,256]{2,0,1:T(4,128)S(1)}, f32[3,90,256]{2,0,1:T(4,128)S(1)}, u32[]{:S(2)}, u32[]{:S(2)}) %collective-permute-start.3) | collective-permute-done | bytes 276512 | tf_op jit(solution)/shard_map/ppermute | solution.py:33
  206.6 3.8 %pad_maximum_fusion.1 = f32[3,90,4608]{2,0,1:T(4,128)} fusion(f32[3,90,256]{2,0,1:T(4,128)S(1)} %collective-permute-done.3, f32[3,90,4096]{2,0,1:T(4,128)S(1)} %fusion.32, f32[3,90,256]{2,0,1:T(4,128)S(1)} %collective-permute-done.2), kind=kLoop, calls=%fused_computation.15 | loop fusion | flops 2488320 | bytes 9953280 | tf_op jit(solution)/shard_map/concatenate | solution.py:29
  210.3 11.3 %copy.14 = f32[3,90,4608]{1,0,2:T(4,128)} copy(f32[3,90,4608]{2,0,1:T(4,128)} %pad_maximum_fusion.1) | data formatting | bytes 9953280 | tf_op jit(solution)/shard_map/concatenate | solution.py:29
  221.6 33.7 %gather_fusion.1 = f32[4096,3,90]{2,1,0:T(4,128)} fusion(f32[3,90,4608]{1,0,2:T(4,128)} %copy.14, s32[4096]{0:T(1024)S(1)} %fusion.88), kind=kCustom, calls=%fused_computation.1.clone | custom fusion | bytes 8863744 | tf_op jit(solution)/shard_map/jit(_take)/gather | solution.py:83
  255.3 10.7 %copy.15 = f32[4096,3,90]{0,1,2:T(4,128)} copy(f32[4096,3,90]{2,1,0:T(4,128)} %gather_fusion.1) | data formatting | bytes 8847360 | tf_op jit(solution)/shard_map/jit(_take)/gather | solution.py:83
  266.0 43.7 %fusion.7 = f32[3,90,4096]{2,0,1:T(4,128)S(1)} fusion(f32[3,90,4096]{2,0,1:T(4,128)} %copy-done.1, f32[3,90,256]{2,0,1:T(4,128)S(1)} %collective-permute-done.3, f32[3,90,256]{2,0,1:T(4,128)S(1)} %collective-permute-done.2, f32[4096,3,90]{0,1,2:T(4,128)} %copy.15, f32[3,89,4096]{2,0,1:T(4,128)} %fusion.54, f32[4096]{0:T(1024)S(1)} %broadcast_select_fusion, ...), kind=kLoop, calls=%fused_computation.23 | loop fusion | flops 37601280 | bytes 18399232 | tf_op jit(solution)/shard_map/add | solution.py:130
  309.7 2.5 copy.28
  312.9 9.4 %copy.16 = f32[1,3,90,4096]{3,0,2,1:T(1,128)} copy(f32[1,3,90,4096]{3,1,2,0:T(4,128)} %fusion.78) | data formatting | bytes 8847360 | tf_op jit(solution)/shard_map/scatter-add | solution.py:131
  (71 shorter events, 17.1 us)
Async XLA Ops:
  0.0 9.2 %copy-start.11 = (s32[4096]{0:T(1024)S(1)}, s32[4096]{0:T(1024)}, u32[]{:S(2)}) copy-start(s32[4096]{0:T(1024)} %param.16) | copy-start | bytes 49156
  0.0 35.2 %copy-start.12 = (s32[1,1,4]{2,1,0:T(1,128)S(1)}, s32[1,1,4]{2,1,0:T(1,128)}, u32[]{:S(2)}) copy-start(s32[1,1,4]{2,1,0:T(1,128)} %param.18) | copy-start | bytes 52
  0.0 39.6 %copy-start.10 = (s32[1,3,4096]{2,0,1:T(1,128)S(1)}, s32[1,3,4096]{2,0,1:T(1,128)}, u32[]{:S(2)}) copy-start(s32[1,3,4096]{2,0,1:T(1,128)} %param.15) | copy-start | bytes 147460
  0.0 39.6 %slice-start.1 = ((s32[1,3,4096]{2,0,1:T(1,128)}), s32[1,2,4096]{2,0,1:T(1,128)S(1)}, s32[]{:S(2)}) async-start(s32[1,3,4096]{2,0,1:T(1,128)} %param.15), calls=%async_computation.1 | async-start | bytes 65536 | tf_op jit(solution)/shard_map/slice | solution.py:82
  0.0 39.6 %copy-start.3 = (f32[1,3,4096]{2,0,1:T(1,128)S(1)}, f32[1,3,4096]{2,0,1:T(1,128)}, u32[]{:S(2)}) copy-start(f32[1,3,4096]{2,0,1:T(1,128)} %param.14) | copy-start | bytes 147460
  0.0 41.1 %copy-start.13 = (s32[1,1,2]{2,1,0:T(1,128)S(1)}, s32[1,1,2]{2,1,0:T(1,128)}, u32[]{:S(2)}) copy-start(s32[1,1,2]{2,1,0:T(1,128)} %param.19) | copy-start | bytes 28
  0.0 42.5 %slice-start = ((f32[1,90,4096]{2,0,1:T(1,128)}), f32[1,89,4096]{2,0,1:T(1,128)S(1)}, s32[]{:S(2)}) async-start(f32[1,90,4096]{2,0,1:T(1,128)} %param.13), calls=%async_computation | async-start | bytes 2916352 | tf_op jit(solution)/shard_map/slice | solution.py:75
  22.6 35.0 %collective-permute-start.4 = (f32[3,4096]{1,0:T(4,128)}, f32[3,4096]{1,0:T(4,128)}, u32[]{:S(2)}, u32[]{:S(2)}) collective-permute-start(f32[3,4096]{1,0:T(4,128)} %psum.14), channel_id=1, source_target_pairs={{31,0},{0,1},{1,2},{2,3},{3,4},{4,5},{5,6},{6,7},{7,8},{8,9},{9,10... | collective-permute-start | bytes 147464 | tf_op jit(solution)/shard_map/ppermute | solution.py:21
  28.1 50.6 %collective-permute-start = (f32[3,90,256]{2,0,1:T(4,128)}, f32[3,90,256]{2,0,1:T(4,128)S(1)}, u32[]{:S(2)}, u32[]{:S(2)}) collective-permute-start(f32[3,90,256]{2,0,1:T(4,128)} %get-tuple-element.20), channel_id=1, source_target_pairs={{0,1},{1,2},{2,3},{3,4},{4,5},{5,6},{6,7},{7,8},{8,9},{9,10},{10,1... | collective-permute-start | bytes 829448 | tf_op jit(solution)/shard_map/ppermute | solution.py:31
  28.6 50.0 %collective-permute-start.1 = (f32[3,90,256]{2,0,1:T(4,128)}, f32[3,90,256]{2,0,1:T(4,128)}, u32[]{:S(2)}, u32[]{:S(2)}) collective-permute-start(f32[3,90,256]{2,0,1:T(4,128)} %get-tuple-element.21), channel_id=1, source_target_pairs={{1,0},{2,1},{3,2},{4,3},{5,4},{6,5},{7,6},{8,7},{9,8},{10,9},{11,1... | collective-permute-start | bytes 829448 | tf_op jit(solution)/shard_map/ppermute | solution.py:33
  42.5 2.7 copy-start
  45.2 5.5 %copy-start.2 = (f32[1,2,256,256]{3,2,1,0:T(8,128)S(1)}, f32[1,2,256,256]{3,2,1,0:T(8,128)}, u32[]{:S(2)}) copy-start(f32[1,2,256,256]{3,2,1,0:T(8,128)} %param.17) | copy-start | bytes 1572868
  60.6 4.3 %collective-permute-start.5 = (f32[2,4096]{1,0:T(2,128)S(1)}, f32[2,4096]{1,0:T(2,128)S(1)}, u32[]{:S(2)}, u32[]{:S(2)}) collective-permute-start(f32[2,4096]{1,0:T(2,128)S(1)} %dynamic_update_slice.14), channel_id=1, source_target_pairs={{1,0},{2,1},{3,2},{4,3},{5,4},{6,5},{7,6},{8,7},{9,8},{10,9},{11,1... | collective-permute-start | bytes 98312 | tf_op jit(solution)/shard_map/ppermute | solution.py:21
  130.8 10.8 %copy-start.4 = (f32[1,1,4096]{2,0,1:T(1,128)S(1)}, f32[1,1,4096]{2,0,1:T(1,128)}, u32[]{:S(2)}) copy-start(f32[1,1,4096]{2,0,1:T(1,128)} %get-tuple-element.27) | copy-start | bytes 49156
  130.8 10.8 %copy-start.5 = (f32[1,1,4096]{2,0,1:T(1,128)S(1)}, f32[1,1,4096]{2,0,1:T(1,128)}, u32[]{:S(2)}) copy-start(f32[1,1,4096]{2,0,1:T(1,128)} %get-tuple-element.28) | copy-start | bytes 49156
  130.8 10.8 %copy-start.6 = (f32[1,1,4096]{2,0,1:T(1,128)S(1)}, f32[1,1,4096]{2,0,1:T(1,128)}, u32[]{:S(2)}) copy-start(f32[1,1,4096]{2,0,1:T(1,128)} %get-tuple-element.29) | copy-start | bytes 49156
  130.8 10.8 %copy-start.7 = (f32[1,1,4096]{2,0,1:T(1,128)S(1)}, f32[1,1,4096]{2,0,1:T(1,128)}, u32[]{:S(2)}) copy-start(f32[1,1,4096]{2,0,1:T(1,128)} %get-tuple-element.30) | copy-start | bytes 49156
  130.8 10.8 %copy-start.8 = (f32[1,1,4096]{2,0,1:T(1,128)S(1)}, f32[1,1,4096]{2,0,1:T(1,128)}, u32[]{:S(2)}) copy-start(f32[1,1,4096]{2,0,1:T(1,128)} %get-tuple-element.31) | copy-start | bytes 49156
  130.8 10.8 %copy-start.9 = (f32[1,1,4096]{2,0,1:T(1,128)S(1)}, f32[1,1,4096]{2,0,1:T(1,128)}, u32[]{:S(2)}) copy-start(f32[1,1,4096]{2,0,1:T(1,128)} %get-tuple-element.32) | copy-start | bytes 49156
  187.5 19.0 %copy-start.1 = (f32[3,90,4096]{2,0,1:T(4,128)}, f32[3,90,4096]{2,0,1:T(4,128)S(1)}, u32[]{:S(2)}) copy-start(f32[3,90,4096]{2,0,1:T(4,128)S(1)} %fusion.32) | copy-start | bytes 13271044
  187.7 15.2 %collective-permute-start.2 = (f32[3,90,256]{2,0,1:T(4,128)S(1)}, f32[3,90,256]{2,0,1:T(4,128)S(1)}, u32[]{:S(2)}, u32[]{:S(2)}) collective-permute-start(f32[3,90,256]{2,0,1:T(4,128)S(1)} %get-tuple-element.18), channel_id=1, source_target_pairs={{0,1},{1,2},{2,3},{3,4},{4,5},{5,6},{6,7},{7,8},{8,9},{9,10},{10,1... | collective-permute-start | bytes 829448 | tf_op jit(solution)/shard_map/ppermute | solution.py:31
  187.8 18.8 %collective-permute-start.3 = (f32[3,90,256]{2,0,1:T(4,128)S(1)}, f32[3,90,256]{2,0,1:T(4,128)S(1)}, u32[]{:S(2)}, u32[]{:S(2)}) collective-permute-start(f32[3,90,256]{2,0,1:T(4,128)S(1)} %get-tuple-element.19), channel_id=1, source_target_pairs={{1,0},{2,1},{3,2},{4,3},{5,4},{6,5},{7,6},{8,7},{9,8},{10,9},{11,1... | collective-permute-start | bytes 829448 | tf_op jit(solution)/shard_map/ppermute | solution.py:33
where the time goes:
time: 324 us; the launch traced here: 322 us
  local copies, waits for them, and re-layouts  141 us (44%)
  other arithmetic  114 us (35%)
  blocking collectives  25.7 us (8%)
  starting transfers between devices  18.3 us (6%)
  waiting for transfers between devices  11.1 us (3%)
  between operations  7.61 us (2%)
  matrix products  4.62 us (1%)
    add x2, other arithmetic, per_device(): current = current + (horizontal + vertical_term(current, mixing)) * scale  89.7 us
    gather x4, local copies, waits for them, and re-layouts, neighbour_mix(): mixed = weights[2][None, None, :] * jnp.take(source, positions[2], axis=2)  88.8 us
    concatenate x2, local copies, waits for them, and re-layouts, with_halo(): jnp.concatenate([lax.ppermute(tail, axis, [(i, (i + 1) % count) for i in...  22.6 us
    unnamed x31, local copies, waits for them, and re-layouts  14.3 us
    ppermute x2, starting transfers between devices, with_halo(): lax.ppermute(head, axis, [((i + 1) % count, i) for i in range(count)])  13.8 us
    psum x1, blocking collectives, per_device(): ocean_flux = lax.psum(ocean_terms[0] + moved, 'group')  13.1 us
    psum x1, blocking collectives, from_root(): return lax.psum(kept, axis)  12.6 us
    concatenate x2, other arithmetic, with_halo(): jnp.concatenate([lax.ppermute(tail, axis, [(i, (i + 1) % count) for i in...  10.9 us
  transfers between devices with their start and end apart: 6, of which 3 were waited for; matrix products, arithmetic and copies ran while one was open for 7% of the time, Pallas kernels for 0%

commit v1 on v0

v1 whole, which is shorter than its diff:
```python
import functools

import jax
import jax.numpy as jnp
from jax import lax
from jax.experimental import pallas as pl
from jax.experimental.pallas import tpu as pltpu
from jax.sharding import PartitionSpec as P

LANES = 128
LEV = 90
NFLD = 3
ROWS = 32
TOP = 8
RIM = 2
BATCH = 18
SLAB = 12
SLAB_STEP = 10
STRIPS = 3
MESH = pl.DeviceIdType.MESH


def lane_gather(values, index):
    return jnp.take_along_axis(values, index, axis=1, mode="promise_in_bounds")


def window_pair(rows, shift, lane):
    turned = [pltpu.roll(row, lax.rem(LANES - shift, LANES), 1) for row in rows]
    inside = lane < LANES - shift
    return [jnp.where(inside, turned[i], turned[i + 1]) for i in range(2)]


def placed(parts, first_row, shift, lane, row_of):
    turned = [pltpu.roll(part, shift, 1) for part in parts]
    late = lane >= shift
    zero = jnp.zeros_like(turned[0])
    pieces = [
        jnp.where(late, turned[0], zero),
        jnp.where(late, turned[1], turned[0]),
        jnp.where(late, zero, turned[1]),
    ]
    total = jnp.zeros(row_of.shape, jnp.float32)
    for step, piece in enumerate(pieces):
        total = jnp.where(row_of == first_row + step, piece, total)
    return total


def window_kernel(
    n_cells,
    state,
    mixing_hbm,
    weight,
    place,
    sea_int,
    remap,
    offsets,
    live,
    out,
    first,
    second,
    mixing,
    sea_out,
    sea_in,
    flux,
    near_air,
    term_out,
    term_in,
    load_sem,
    halo_send,
    halo_recv,
    sea_send,
    sea_recv,
    term_send,
    term_recv,
):
    cell = lax.axis_index("cells")
    group = lax.axis_index("group")
    right = lax.rem(cell + 1, n_cells)
    left = lax.rem(cell + n_cells - 1, n_cells)
    is_ocean = group == STRIPS

    def levels_of(field):
        return pl.ds(field * LEV, LEV)

    def load_of(field):
        return pltpu.make_async_copy(
            state.at[levels_of(field)],
            first.at[levels_of(field), pl.ds(TOP, ROWS), :],
            load_sem.at[field],
        )

    mixing_copy = pltpu.make_async_copy(mixing_hbm, mixing, load_sem.at[NFLD])
    for field in range(NFLD):
        load_of(field).start()
    mixing_copy.start()

    barrier = pltpu.get_barrier_semaphore()
    for device in (left, right):
        pl.semaphore_signal(barrier, inc=1, device_id=(group, device), device_id_type=MESH)

    @pl.when(is_ocean)
    def _():
        for strip in range(STRIPS):
            for device in (cell, right):
                pl.semaphore_signal(barrier, inc=1, device_id=(strip, device), device_id_type=MESH)
        pl.semaphore_wait(barrier, 2 + 2 * STRIPS)

    @pl.when(jnp.logical_not(is_ocean))
    def _():
        for device in (cell, left):
            pl.semaphore_signal(barrier, inc=1, device_id=(STRIPS, device), device_id_type=MESH)
        pl.semaphore_wait(barrier, 4)

    def halo(step, field, side):
        levels = levels_of(field)
        if step == 0:
            source, low, high, target = state, 0, ROWS - RIM, first
        else:
            source, low, high, target = second, TOP, TOP + ROWS - RIM, second
        if side == 0:
            begin, land, device = high, TOP - RIM, right
        else:
            begin, land, device = low, TOP + ROWS, left
        return pltpu.make_async_remote_copy(
            src_ref=source.at[levels, pl.ds(begin, RIM), :],
            dst_ref=target.at[levels, pl.ds(land, RIM), :],
            send_sem=halo_send.at[step, side, field],
            recv_sem=halo_recv.at[step, side, field],
            device_id=(group, device),
            device_id_type=MESH,
        )

    for field in range(NFLD):
        for side in range(2):
            halo(0, field, side).start()

    def sea_copy(strip, pair):
        return pltpu.make_async_remote_copy(
            src_ref=sea_out.at[:, pl.ds(strip * SLAB_STEP, SLAB), :],
            dst_ref=sea_in.at[pair, :, pl.ds(0, SLAB), :],
            send_sem=sea_send.at[strip, pair],
            recv_sem=sea_recv.at[pair],
            device_id=(strip, (cell, right)[pair]),
            device_id_type=MESH,
        )

    def term_copy(strip, pair):
        return pltpu.make_async_remote_copy(
            src_ref=term_out.at[pair],
            dst_ref=term_in.at[strip, pair],
            send_sem=term_send.at[pair],
            recv_sem=term_recv.at[strip, pair],
            device_id=(STRIPS, (cell, left)[pair]),
            device_id_type=MESH,
        )

    sea_mask = sea_int[...].astype(jnp.float32)
    for field in range(NFLD):
        load_of(field).wait()
    mixing_copy.wait()

    @pl.when(is_ocean)
    def _():
        for field in range(2):
            sea_out[field] = first[field * LEV, TOP : TOP + ROWS, :] * sea_mask
        sea_out[2] = sea_mask
        for strip in range(STRIPS):
            for pair in range(2):
                sea_copy(strip, pair).start()

    lane8 = lax.broadcasted_iota(jnp.int32, (8, LANES), 1)
    row8 = lax.broadcasted_iota(jnp.int32, (8, LANES), 0)
    half = lane8 < LANES // 2

    def advance(source, target, target_top, field, chunk):
        rows = slice(chunk * 8, chunk * 8 + 8)
        position = [place[k, rows, :] for k in range(3)]
        index = [p & (LANES - 1) for p in position]
        apart = [(p >> 7) - (row8 + (chunk * 8 + RIM)) for p in position]
        part = [weight[k, rows, :] for k in range(3)]
        centre = part[0] + part[1] + part[2]
        scale = jnp.where(is_ocean, sea_int[rows, :].astype(jnp.float32), 1.0)
        far_at = [apart[2] == g for g in (-2, -1, 1, 2)]
        here = [apart[k] == 0 for k in range(2)]
        base = TOP + chunk * 8
        steps = LEV // BATCH

        def batch(t, carry):
            begin, below = carry
            level = t * BATCH
            at = field * LEV + level
            x = [begin] + [source[at + b, pl.ds(base, 8), :] for b in range(1, BATCH + 1)]
            before = [source[at + b, pl.ds(base - 1, 8), :] for b in range(BATCH)]
            after = [source[at + b, pl.ds(base + 1, 8), :] for b in range(BATCH)]
            mixed = []
            for b in range(BATCH):
                before2 = source[at + b, pl.ds(base - 2, 8), :]
                after2 = source[at + b, pl.ds(base + 2, 8), :]
                value = lane_gather(x[b], index[2])
                for chosen, row in zip(far_at, (before2, before[b], after[b], after2)):
                    value = jnp.where(chosen, lane_gather(row, index[2]), value)
                mixed.append(part[2] * value - centre * x[b])
            edge = [jnp.where(half, after[b], before[b]) for b in range(BATCH)]
            for k in range(2):
                for b in range(BATCH):
                    value = jnp.where(here[k], lane_gather(x[b], index[k]), lane_gather(edge[b], index[k]))
                    mixed[b] = mixed[b] + part[k] * value
            for b in range(BATCH):
                upward = mixing[level + b, rows, :] * (x[b + 1] - x[b])
                if b == BATCH - 1:
                    upward = jnp.where(t == steps - 1, 0.0, upward)
                target[at + b, target_top + chunk * 8 : target_top + chunk * 8 + 8, :] = x[b] + scale * (
                    mixed[b] + (upward - below)
                )
                below = upward
            return x[BATCH], below

        start = source[field * LEV, pl.ds(base, 8), :]
        lax.fori_loop(0, steps, batch, (start, jnp.zeros((8, LANES), jnp.float32)))

    def each_field(body):
        lax.fori_loop(0, NFLD, lambda field, c: (body(field), c)[1], 0)

    def inner_first(field):
        for chunk in (1, 2):
            advance(first, second, TOP, field, chunk)

    each_field(inner_first)

    lane1 = lax.broadcasted_iota(jnp.int32, (1, LANES), 1)
    lane3 = lax.broadcasted_iota(jnp.int32, (3, LANES), 1)
    lane2 = lax.broadcasted_iota(jnp.int32, (2, LANES), 1)
    row_of = lax.broadcasted_iota(jnp.int32, (ROWS, LANES), 0)
    slab_row = lax.broadcasted_iota(jnp.int32, (16, LANES), 0)

    @pl.when(jnp.logical_not(is_ocean))
    def _():
        gap = [jnp.zeros((ROWS, LANES), jnp.float32) for _ in range(2)]
        for field in range(2):
            near_air[field, 0:ROWS, :] = first[field * LEV, TOP : TOP + ROWS, :]
            near_air[field, ROWS:, :] = jnp.zeros((8, LANES), jnp.float32)
        for pair in range(2):
            sea_copy(0, pair).wait_recv()
        for pair in range(2):
            col = offsets[2 * pair]
            row = offsets[2 * pair + 1] - group * (SLAB_STEP * LANES)
            rows_live = live[pair]
            sea = window_pair(
                [sea_in[pair, :, jnp.clip((row >> 7) + i, 0, 15), :] for i in range(3)],
                row & (LANES - 1),
                lane3,
            )
            sea = [jnp.where(lane3 + i * LANES < rows_live, sea[i], 0.0) for i in range(2)]
            moved = jnp.zeros((3, 2 * LANES), jnp.float32)
            for i in range(2):
                moved = moved + jnp.dot(
                    sea[i],
                    remap[pair, i * LANES : (i + 1) * LANES, :],
                    precision=lax.Precision.HIGHEST,
                    preferred_element_type=jnp.float32,
                )
            for field in range(2):
                air = window_pair(
                    [near_air[field, pl.ds(jnp.clip((col >> 7) + i, 0, ROWS), 1), :] for i in range(3)],
                    col & (LANES - 1),
                    lane1,
                )
                parts = [
                    moved[field : field + 1, i * LANES : (i + 1) * LANES]
                    - air[i] * moved[2:3, i * LANES : (i + 1) * LANES]
                    for i in range(2)
                ]
                gap[field] = gap[field] + placed(parts, col >> 7, col & (LANES - 1), lane1, row_of)
        for field in range(2):
            flux[field, 0:ROWS, :] = 0.5 * gap[field]
            flux[field, ROWS:, :] = jnp.zeros((8, LANES), jnp.float32)
        for pair in range(2):
            col = offsets[2 * pair]
            row = offsets[2 * pair + 1] - group * (SLAB_STEP * LANES)
            rows_live = live[pair]
            back = window_pair(
                [flux[:, jnp.clip((col >> 7) + i, 0, ROWS), :] for i in range(3)], col & (LANES - 1), lane2
            )
            parts = []
            for i in range(2):
                block = remap[pair, i * LANES : (i + 1) * LANES, :]
                term = jnp.zeros((2, LANES), jnp.float32)
                for j in range(2):
                    term = term + lax.dot_general(
                        back[j],
                        block[:, j * LANES : (j + 1) * LANES],
                        (((1,), (1,)), ((), ())),
                        precision=lax.Precision.HIGHEST,
                        preferred_element_type=jnp.float32,
                    )
                parts.append(jnp.where(lane2 + i * LANES < rows_live, term, 0.0))
            for field in range(2):
                laid = placed(
                    [part[field : field + 1] for part in parts], row >> 7, row & (LANES - 1), lane1, slab_row
                )
                term_out[pair, field] = laid
        for strip in range(STRIPS):

            @pl.when(group == strip)
            def _():
                for pair in range(2):
                    term_copy(strip, pair).start()

    def outer_first(field):
        for side, chunk in ((0, 0), (1, ROWS // 8 - 1)):
            halo(0, field, side).wait_recv()
            advance(first, second, TOP, field, chunk)
            halo(1, field, 1 - side).start()

    each_field(outer_first)

    def inner_second(field):
        for chunk in (1, 2):
            advance(second, out, 0, field, chunk)

    each_field(inner_second)

    @pl.when(is_ocean)
    def _():
        for field in range(2):
            flux[field] = jnp.zeros((ROWS + 8, LANES), jnp.float32)
        for strip in range(STRIPS):
            for pair in range(2):
                term_copy(strip, pair).wait_recv()
                for field in range(2):
                    at = slice(strip * SLAB_STEP, strip * SLAB_STEP + SLAB)
                    flux[field, at, :] = flux[field, at, :] + term_in[strip, pair, field, 0:SLAB, :]
        for field in range(2):
            flux[field, 0:ROWS, :] = -flux[field, 0:ROWS, :] * sea_mask

    def outer_second(field):
        for side, chunk in ((0, 0), (1, ROWS // 8 - 1)):
            halo(1, field, side).wait_recv()
            advance(second, out, 0, field, chunk)

    each_field(outer_second)
    for field in range(2):
        out[field * LEV] = out[field * LEV] + flux[field, 0:ROWS, :]

    for step in range(2):
        for field in range(NFLD):
            for side in range(2):
                halo(step, field, side).wait_send()

    @pl.when(is_ocean)
    def _():
        for strip in range(STRIPS):
            for pair in range(2):
                sea_copy(strip, pair).wait_send()

    @pl.when(jnp.logical_not(is_ocean))
    def _():
        for pair in range(2):
            term_copy(0, pair).wait_send()


def per_device(
    n_cells,
    state,
    vertical_mix,
    neighbour_weight,
    neighbours,
    land_sea,
    remap_weight,
    pair_offsets,
    pair_rows,
):
    any_space = pl.BlockSpec(memory_space=pl.ANY)
    vmem = pl.BlockSpec(memory_space=pltpu.VMEM)
    smem = pl.BlockSpec(memory_space=pltpu.SMEM)
    levels = NFLD * LEV
    f32 = jnp.float32
    dma = pltpu.SemaphoreType.DMA
    out = pl.pallas_call(
        functools.partial(window_kernel, n_cells),
        out_shape=jax.ShapeDtypeStruct((levels, ROWS, LANES), f32),
        in_specs=[any_space, any_space, vmem, vmem, vmem, vmem, smem, smem],
        out_specs=vmem,
        scratch_shapes=[
            pltpu.VMEM((levels + 2, 48, LANES), f32),
            pltpu.VMEM((levels + 2, 48, LANES), f32),
            pltpu.VMEM((LEV, ROWS, LANES), f32),
            pltpu.VMEM((3, ROWS, LANES), f32),
            pltpu.VMEM((2, 3, 16, LANES), f32),
            pltpu.VMEM((2, ROWS + 8, LANES), f32),
            pltpu.VMEM((2, ROWS + 8, LANES), f32),
            pltpu.VMEM((2, 2, 16, LANES), f32),
            pltpu.VMEM((STRIPS, 2, 2, 16, LANES), f32),
            dma((NFLD + 1,)),
            dma((2, 2, NFLD)),
            dma((2, 2, NFLD)),
            dma((STRIPS, 2)),
            dma((2,)),
            dma((2,)),
            dma((STRIPS, 2)),
        ],
        compiler_params=pltpu.CompilerParams(
            collective_id=0, has_side_effects=True, vmem_limit_bytes=48 * 1024 * 1024
        ),
        name="window",
    )(
        state.reshape(levels, ROWS, LANES),
        vertical_mix.reshape(LEV, ROWS, LANES),
        neighbour_weight.reshape(3, ROWS, LANES),
        neighbours.reshape(3, ROWS, LANES),
        land_sea.reshape(ROWS, LANES),
        remap_weight[0],
        pair_offsets.reshape(4),
        pair_rows.reshape(2),
    )
    return out.reshape(1, NFLD, LEV, ROWS * LANES)


def solution(mesh):
    return jax.shard_map(
        functools.partial(per_device, mesh.shape["cells"]),
        mesh=mesh,
        in_specs=(
            P("group", None, None, "cells"),
            P("group", None, "cells"),
            P("group", None, "cells"),
            P("group", None, "cells"),
            P("cells"),
            P("group", None, "cells", None),
            P("group", "cells", None),
            P("group", "cells", None),
        ),
        out_specs=P("group", None, None, "cells"),
        check_vma=False,
    )
```

time: 324 us -> 69.3 us (0.21)
  local copies, waits for them, and re-layouts: 141 us -> 14.4 us
  other arithmetic: 114 us -> 0 us
  Pallas kernels: 0 us -> 54.5 us
  blocking collectives: 25.7 us -> 0 us
  starting transfers between devices: 18.3 us -> 0 us
  waiting for transfers between devices: 11.1 us -> 0 us
  between operations: 7.61 us -> 0.02 us
  matrix products: 4.62 us -> 0 us
    add x5 -> x0, other arithmetic: 90.5 us -> none  [the longest x2 89.7 us: per_device(): current = current + (horizontal + vertical_term(current, mixing)) * scale]
    gather x4 -> x0, local copies, waits for them, and re-layouts: 88.8 us -> none  [neighbour_mix(): mixed = weights[2][None, None, :] * jnp.take(source, positions[2], axis=2)]
    pallas_call x0 -> x1, Pallas kernels: none -> 54.5 us  [per_device(): pl.pallas_call(functools.partial(window_kernel, n_cells), out_shape=jax.S...]
    psum x2 -> x0, blocking collectives: 25.7 us -> none  [the longest x1 13.1 us: per_device(): ocean_flux = lax.psum(ocean_terms[0] + moved, 'group')]
    concatenate x2 -> x0, local copies, waits for them, and re-layouts: 22.6 us -> none  [with_halo(): jnp.concatenate([lax.ppermute(tail, axis, [(i, (i + 1) % count) for i in...]
    ppermute x6 -> x0, starting transfers between devices: 18.3 us -> none  [the longest x2 13.8 us: with_halo(): lax.ppermute(head, axis, [((i + 1) % count, i) for i in range(count)])]
    ppermute x6 -> x0, waiting for transfers between devices: 11.1 us -> none  [the longest x2 3.83 us: passed_along(): return lax.ppermute(block, axis, route)]
    concatenate x2 -> x0, other arithmetic: 10.9 us -> none  [with_halo(): jnp.concatenate([lax.ppermute(tail, axis, [(i, (i + 1) % count) for i in...]
  transfers between devices with their start and end apart: 6 -> 0, of which waited for: 3 -> 0; matrix products, arithmetic and copies ran while one was open for 7% -> 0% of each run, Pallas kernels for 0% -> 0%
where the time goes in v1:
time: 69.3 us; the launch traced here: 68.9 us
  Pallas kernels  54.5 us (79%)
  local copies, waits for them, and re-layouts  14.4 us (21%)
    pallas_call x1, Pallas kernels, per_device(): pl.pallas_call(functools.partial(window_kernel, n_cells), out_shape=jax.S...  54.5 us
    unnamed x15, local copies, waits for them, and re-layouts  14.4 us

profile of v1, /device:TPU:1, one launch (start us, length us, event | category | flops | bytes accessed | tf_op | source)
XLA Modules:
  0.0 68.9 jit_solution(12242063797407933639)
XLA Ops:
  0.0 0.0 copy-start
  0.0 1.4 %copy-done = f32[1,90,4096]{2,0,1:T(1,128)S(1)} copy-done((f32[1,90,4096]{2,0,1:T(1,128)S(1)}, f32[1,90,4096]{2,0,1:T(1,128)}, u32[]{:S(2)}) %copy-start) | copy-done | bytes 1474584
  1.4 0.0 copy-start.1
  1.4 1.0 %copy-done.1 = f32[1,2,256,256]{3,2,1,0:T(8,128)S(1)} copy-done((f32[1,2,256,256]{3,2,1,0:T(8,128)S(1)}, f32[1,2,256,256]{3,2,1,0:T(8,128)}, u32[]{:S(2)}) %copy-start.1) | copy-done | bytes 524312
  2.4 0.0 copy-start.2
  2.4 0.8 %copy-done.2 = f32[1,3,4096]{2,0,1:T(1,128)S(1)} copy-done((f32[1,3,4096]{2,0,1:T(1,128)S(1)}, f32[1,3,4096]{2,0,1:T(1,128)}, u32[]{:S(2)}) %copy-start.2) | copy-done | bytes 49176
  3.2 0.0 copy-start.3
  3.2 0.8 %copy-done.3 = s32[1,3,4096]{2,0,1:T(1,128)S(1)} copy-done((s32[1,3,4096]{2,0,1:T(1,128)S(1)}, s32[1,3,4096]{2,0,1:T(1,128)}, u32[]{:S(2)}) %copy-start.3) | copy-done | bytes 49176
  4.0 0.0 copy-start.4
  4.0 0.7 %copy-done.4 = s32[4096]{0:T(1024)S(1)} copy-done((s32[4096]{0:T(1024)S(1)}, s32[4096]{0:T(1024)}, u32[]{:S(2)}) %copy-start.4) | copy-done | bytes 16408
  4.7 0.0 copy-start.5
  4.7 0.7 copy-done.5
  5.4 0.0 copy-start.6
  5.4 0.7 copy-done.6
  6.0 54.5 %window.1 = f32[270,32,128]{2,1,0:T(8,128)} custom-call(f32[270,32,128]{2,1,0:T(8,128)} %bitcast.17, f32[90,32,128]{2,1,0:T(8,128)S(1)} %bitcast.9, f32[3,32,128]{2,1,0:T(8,128)S(1)} %bitcast.11, s32[3,32,128]{2,1,0:T(8,128)S(1)} %bitcast.12, s32[32,128]{1,0:T(8,128)S(1)} %bitcast.13, f32[2,256,256]{2,1,0:T(8,128)S(1)} %bitcast.10, s32[4]{0:T(128)S(1)} %bitcast.14, ...), custom_call_target="tpu_custom_call" | custom-call | tf_op jit(solution)/shard_map/window/pallas_call | solution.py:379
  60.6 8.4 %copy.12 = f32[1,3,90,4096]{3,0,2,1:T(1,128)} copy(f32[1,3,90,4096]{3,0,2,1:T(1,128)} %bitcast.16) | data formatting | bytes 8847360
Async XLA Ops:
  0.0 1.4 %copy-start = (f32[1,90,4096]{2,0,1:T(1,128)S(1)}, f32[1,90,4096]{2,0,1:T(1,128)}, u32[]{:S(2)}) copy-start(f32[1,90,4096]{2,0,1:T(1,128)} %param.9) | copy-start | bytes 4423684
  1.4 1.0 %copy-start.1 = (f32[1,2,256,256]{3,2,1,0:T(8,128)S(1)}, f32[1,2,256,256]{3,2,1,0:T(8,128)}, u32[]{:S(2)}) copy-start(f32[1,2,256,256]{3,2,1,0:T(8,128)} %param.13) | copy-start | bytes 1572868
  2.4 0.8 %copy-start.2 = (f32[1,3,4096]{2,0,1:T(1,128)S(1)}, f32[1,3,4096]{2,0,1:T(1,128)}, u32[]{:S(2)}) copy-start(f32[1,3,4096]{2,0,1:T(1,128)} %param.10) | copy-start | bytes 147460
  3.2 0.8 %copy-start.3 = (s32[1,3,4096]{2,0,1:T(1,128)S(1)}, s32[1,3,4096]{2,0,1:T(1,128)}, u32[]{:S(2)}) copy-start(s32[1,3,4096]{2,0,1:T(1,128)} %param.11) | copy-start | bytes 147460
  4.0 0.7 %copy-start.4 = (s32[4096]{0:T(1024)S(1)}, s32[4096]{0:T(1024)}, u32[]{:S(2)}) copy-start(s32[4096]{0:T(1024)} %param.12) | copy-start | bytes 49156
  4.7 0.7 copy-start.5
  5.4 0.7 copy-start.6

commit v2 on v1

--- a/solution.py
+++ b/solution.py
@@ -13,7 +13,7 @@
 ROWS = 32
 TOP = 8
 RIM = 2
-BATCH = 18
+BATCH = 30
 SLAB = 12
 SLAB_STEP = 10
 STRIPS = 3
@@ -49,19 +49,25 @@
     n_cells,
     state,
     mixing_hbm,
+    weight_hbm,
+    place_hbm,
+    sea_hbm,
+    remap_hbm,
+    offsets_hbm,
+    live_hbm,
+    out,
+    flux,
     weight,
     place,
     sea_int,
     remap,
     offsets,
     live,
-    out,
     first,
     second,
     mixing,
     sea_out,
     sea_in,
-    flux,
     near_air,
     term_out,
     term_in,
@@ -89,10 +95,16 @@
             load_sem.at[field],
         )
 
-    mixing_copy = pltpu.make_async_copy(mixing_hbm, mixing, load_sem.at[NFLD])
+    surface = (sea_hbm, sea_int), (place_hbm, place), (weight_hbm, weight), (mixing_hbm, mixing)
+    coupling = (remap_hbm, remap), (offsets_hbm, offsets), (live_hbm, live)
+    others = [
+        pltpu.make_async_copy(source, target, load_sem.at[NFLD + i])
+        for i, (source, target) in enumerate(surface + coupling)
+    ]
     for field in range(NFLD):
         load_of(field).start()
-    mixing_copy.start()
+    for copy in others:
+        copy.start()
 
     barrier = pltpu.get_barrier_semaphore()
     for device in (left, right):
@@ -154,10 +166,11 @@
             device_id_type=MESH,
         )
 
-    sea_mask = sea_int[...].astype(jnp.float32)
     for field in range(NFLD):
         load_of(field).wait()
-    mixing_copy.wait()
+    for copy in others:
+        copy.wait()
+    sea_mask = sea_int[...].astype(jnp.float32)
 
     @pl.when(is_ocean)
     def _():
@@ -339,8 +352,6 @@
             advance(second, out, 0, field, chunk)
 
     each_field(outer_second)
-    for field in range(2):
-        out[field * LEV] = out[field * LEV] + flux[field, 0:ROWS, :]
 
     for step in range(2):
         for field in range(NFLD):
@@ -357,6 +368,23 @@
     def _():
         for pair in range(2):
             term_copy(0, pair).wait_send()
+
+
+def store_kernel(fields, forcing, out, top, sem):
+    copies = []
+    for field in range(NFLD):
+        first = field * LEV + (1 if field < 2 else 0)
+        rows = pl.ds(first, (field + 1) * LEV - first)
+        copies.append(pltpu.make_async_copy(fields.at[rows], out.at[rows], sem.at[field]))
+    for copy in copies:
+        copy.start()
+    for field in range(2):
+        top[field] = fields[field * LEV] + forcing[field, 0:ROWS, :]
+        copy = pltpu.make_async_copy(top.at[field], out.at[field * LEV], sem.at[NFLD + field])
+        copy.start()
+        copies.append(copy)
+    for copy in copies:
+        copy.wait()
 
 
 def per_device(
@@ -370,40 +398,12 @@
     pair_offsets,
     pair_rows,
 ):
-    any_space = pl.BlockSpec(memory_space=pl.ANY)
+    hbm = pl.BlockSpec(memory_space=pltpu.HBM)
     vmem = pl.BlockSpec(memory_space=pltpu.VMEM)
-    smem = pl.BlockSpec(memory_space=pltpu.SMEM)
     levels = NFLD * LEV
     f32 = jnp.float32
     dma = pltpu.SemaphoreType.DMA
-    out = pl.pallas_call(
-        functools.partial(window_kernel, n_cells),
-        out_shape=jax.ShapeDtypeStruct((levels, ROWS, LANES), f32),
-        in_specs=[any_space, any_space, vmem, vmem, vmem, vmem, smem, smem],
-        out_specs=vmem,
-        scratch_shapes=[
-            pltpu.VMEM((levels + 2, 48, LANES), f32),
-            pltpu.VMEM((levels + 2, 48, LANES), f32),
-            pltpu.VMEM((LEV, ROWS, LANES), f32),
-            pltpu.VMEM((3, ROWS, LANES), f32),
-            pltpu.VMEM((2, 3, 16, LANES), f32),
-            pltpu.VMEM((2, ROWS + 8, LANES), f32),
-            pltpu.VMEM((2, ROWS + 8, LANES), f32),
-            pltpu.VMEM((2, 2, 16, LANES), f32),
-            pltpu.VMEM((STRIPS, 2, 2, 16, LANES), f32),
-            dma((NFLD + 1,)),
-            dma((2, 2, NFLD)),
-            dma((2, 2, NFLD)),
-            dma((STRIPS, 2)),
-            dma((2,)),
-            dma((2,)),
-            dma((STRIPS, 2)),
-        ],
-        compiler_params=pltpu.CompilerParams(
-            collective_id=0, has_side_effects=True, vmem_limit_bytes=48 * 1024 * 1024
-        ),
-        name="window",
-    )(
+    operands = (
         state.reshape(levels, ROWS, LANES),
         vertical_mix.reshape(LEV, ROWS, LANES),
         neighbour_weight.reshape(3, ROWS, LANES),
@@ -413,6 +413,47 @@
         pair_offsets.reshape(4),
         pair_rows.reshape(2),
     )
+    fields, forcing = pl.pallas_call(
+        functools.partial(window_kernel, n_cells),
+        out_shape=(pltpu.VMEM((levels, ROWS, LANES), f32), pltpu.VMEM((2, ROWS + 8, LANES), f32)),
+        in_specs=[hbm] * 8,
+        out_specs=(vmem, vmem),
+        scratch_shapes=[
+            pltpu.VMEM((3, ROWS, LANES), f32),
+            pltpu.VMEM((3, ROWS, LANES), jnp.int32),
+            pltpu.VMEM((ROWS, LANES), jnp.int32),
+            pltpu.VMEM((2, 2 * LANES, 2 * LANES), f32),
+            pltpu.SMEM((4,), jnp.int32),
+            pltpu.SMEM((2,), jnp.int32),
+            pltpu.VMEM((levels + 2, 48, LANES), f32),
+            pltpu.VMEM((levels + 2, 48, LANES), f32),
+            pltpu.VMEM((LEV, ROWS, LANES), f32),
+            pltpu.VMEM((3, ROWS, LANES), f32),
+            pltpu.VMEM((2, 3, 16, LANES), f32),
+            pltpu.VMEM((2, ROWS + 8, LANES), f32),
+            pltpu.VMEM((2, 2, 16, LANES), f32),
+            pltpu.VMEM((STRIPS, 2, 2, 16, LANES), f32),
+            dma((NFLD + 7,)),
+            dma((2, 2, NFLD)),
+            dma((2, 2, NFLD)),
+            dma((STRIPS, 2)),
+            dma((2,)),
+            dma((2,)),
+            dma((STRIPS, 2)),
+        ],
+        compiler_params=pltpu.CompilerParams(
+            collective_id=0, has_side_effects=True, vmem_limit_bytes=40 * 1024 * 1024
+        ),
+        name="window",
+    )(*(pltpu.with_memory_space_constraint(operand, pltpu.HBM) for operand in operands))
+    out = pl.pallas_call(
+        store_kernel,
+        out_shape=jax.ShapeDtypeStruct((levels, ROWS, LANES), f32),
+        in_specs=[vmem, vmem],
+        out_specs=hbm,
+        scratch_shapes=[pltpu.VMEM((2, ROWS, LANES), f32), dma((2 * NFLD,))],
+        name="store",
+    )(fields, forcing)
     return out.reshape(1, NFLD, LEV, ROWS * LANES)
 
 

time: 69.3 us -> 56.2 us (0.81)
  local copies, waits for them, and re-layouts: 14.4 us -> 2.64 us
  Pallas kernels: 54.5 us -> 53.4 us
    unnamed x15 -> x4, local copies, waits for them, and re-layouts: 14.4 us -> 2.64 us
    pallas_call x1 -> x2, Pallas kernels: 54.5 us -> 53.4 us  [the longest x1 49 us: per_device(): pl.pallas_call(functools.partial(window_kernel, n_cells), out_shape=(pltp...]
where the time goes in v2:
time: 56.2 us; the launch traced here: 56.1 us
  Pallas kernels  53.4 us (95%)
  local copies, waits for them, and re-layouts  2.64 us (5%)
    pallas_call x1, Pallas kernels, per_device(): pl.pallas_call(functools.partial(window_kernel, n_cells), out_shape=(pltp...  49 us
    pallas_call x1, Pallas kernels, per_device(): pl.pallas_call(store_kernel, out_shape=jax.ShapeDtypeStruct((levels, ROWS...  4.38 us
    unnamed x4, local copies, waits for them, and re-layouts  2.64 us

profile of v2, /device:TPU:1, one launch (start us, length us, event | category | flops | bytes accessed | tf_op | source)
XLA Modules:
  0.0 56.1 jit_solution(11272985108787646469)
XLA Ops:
  0.0 49.0 %window.1 = (f32[270,32,128]{2,1,0:T(8,128)S(1)}, f32[2,40,128]{2,1,0:T(8,128)S(1)}) custom-call(f32[270,32,128]{2,1,0:T(8,128)} %bitcast.9, f32[90,32,128]{2,1,0:T(8,128)} %bitcast.10, f32[3,32,128]{2,1,0:T(8,128)} %bitcast.12, s32[3,32,128]{2,1,0:T(8,128)} %bitcast.13, s32[32,128]{1,0:T(8,128)} %bitcast.14, f32[2,256,256]{2,1,0:T(8,128)} %bitcast.11, ...), custom_call_target="tpu_custom_call" | custom-call | tf_op jit(solution)/shard_map/window/pallas_call | solution.py:416
  49.0 0.0 copy-start
  49.0 2.0 %copy-done = f32[270,32,128]{2,1,0:T(8,128)} copy-done((f32[270,32,128]{2,1,0:T(8,128)}, f32[270,32,128]{2,1,0:T(8,128)S(1)}, u32[]{:S(2)}) %copy-start) | copy-done | bytes 4423704
  51.1 0.0 copy-start.1
  51.1 0.6 %copy-done.1 = f32[2,40,128]{2,1,0:T(8,128)} copy-done((f32[2,40,128]{2,1,0:T(8,128)}, f32[2,40,128]{2,1,0:T(8,128)S(1)}, u32[]{:S(2)}) %copy-start.1) | copy-done | bytes 40984
  51.7 4.4 %store.1 = f32[270,32,128]{2,1,0:T(8,128)} custom-call(f32[270,32,128]{2,1,0:T(8,128)} %copy-done, f32[2,40,128]{2,1,0:T(8,128)} %copy-done.1), custom_call_target="tpu_custom_call" | custom-call | tf_op jit(solution)/shard_map/store/pallas_call | solution.py:449
Async XLA Ops:
  49.0 2.0 %copy-start = (f32[270,32,128]{2,1,0:T(8,128)}, f32[270,32,128]{2,1,0:T(8,128)S(1)}, u32[]{:S(2)}) copy-start(f32[270,32,128]{2,1,0:T(8,128)S(1)} %get-tuple-element.7.fields) | copy-start | bytes 13271044
  51.1 0.6 %copy-start.1 = (f32[2,40,128]{2,1,0:T(8,128)}, f32[2,40,128]{2,1,0:T(8,128)S(1)}, u32[]{:S(2)}) copy-start(f32[2,40,128]{2,1,0:T(8,128)S(1)} %get-tuple-element.8.forcing) | copy-start | bytes 122884

commit v3 on v2

--- a/solution.py
+++ b/solution.py
@@ -13,7 +13,7 @@
 ROWS = 32
 TOP = 8
 RIM = 2
-BATCH = 30
+BATCH = 45
 SLAB = 12
 SLAB_STEP = 10
 STRIPS = 3
@@ -452,6 +452,7 @@
         in_specs=[vmem, vmem],
         out_specs=hbm,
         scratch_shapes=[pltpu.VMEM((2, ROWS, LANES), f32), dma((2 * NFLD,))],
+        compiler_params=pltpu.CompilerParams(vmem_limit_bytes=2 * 1024 * 1024),
         name="store",
     )(fields, forcing)
     return out.reshape(1, NFLD, LEV, ROWS * LANES)

time: 56.2 us -> 50.3 us (0.90)
  Pallas kernels: 53.4 us -> 50.2 us
  local copies, waits for them, and re-layouts: 2.64 us -> 0 us
    unnamed x4 -> x0, local copies, waits for them, and re-layouts: 2.64 us -> none
    pallas_call x1, Pallas kernels: 4.38 us -> 2.13 us  [per_device(): pl.pallas_call(store_kernel, out_shape=jax.ShapeDtypeStruct((levels, ROWS...]
    pallas_call x1, Pallas kernels: 49 us -> 48.1 us  [per_device(): pl.pallas_call(functools.partial(window_kernel, n_cells), out_shape=(pltp...]
where the time goes in v3:
time: 50.3 us; the launch traced here: 50.2 us
  Pallas kernels  50.2 us (100%)
    pallas_call x1, Pallas kernels, per_device(): pl.pallas_call(functools.partial(window_kernel, n_cells), out_shape=(pltp...  48.1 us
    pallas_call x1, Pallas kernels, per_device(): pl.pallas_call(store_kernel, out_shape=jax.ShapeDtypeStruct((levels, ROWS...  2.13 us

profile of v3, /device:TPU:1, one launch (start us, length us, event | category | flops | bytes accessed | tf_op | source)
XLA Modules:
  0.0 50.2 jit_solution(2736128043376288782)
XLA Ops:
  0.0 48.1 %window.1 = (f32[270,32,128]{2,1,0:T(8,128)S(1)}, f32[2,40,128]{2,1,0:T(8,128)S(1)}) custom-call(f32[270,32,128]{2,1,0:T(8,128)} %bitcast.9, f32[90,32,128]{2,1,0:T(8,128)} %bitcast.10, f32[3,32,128]{2,1,0:T(8,128)} %bitcast.12, s32[3,32,128]{2,1,0:T(8,128)} %bitcast.13, s32[32,128]{1,0:T(8,128)} %bitcast.14, f32[2,256,256]{2,1,0:T(8,128)} %bitcast.11, ...), custom_call_target="tpu_custom_call" | custom-call | tf_op jit(solution)/shard_map/window/pallas_call | solution.py:416
  48.1 2.1 %store.1 = f32[270,32,128]{2,1,0:T(8,128)} custom-call(f32[270,32,128]{2,1,0:T(8,128)S(1)} %get-tuple-element.7.fields, f32[2,40,128]{2,1,0:T(8,128)S(1)} %get-tuple-element.8.forcing), custom_call_target="tpu_custom_call" | custom-call | tf_op jit(solution)/shard_map/store/pallas_call | solution.py:449

commit v4 on v3

--- a/solution.py
+++ b/solution.py
@@ -65,6 +65,7 @@
     live,
     first,
     second,
+    rims,
     mixing,
     sea_out,
     sea_in,
@@ -95,15 +96,22 @@
             load_sem.at[field],
         )
 
-    surface = (sea_hbm, sea_int), (place_hbm, place), (weight_hbm, weight), (mixing_hbm, mixing)
-    coupling = (remap_hbm, remap), (offsets_hbm, offsets), (live_hbm, live)
-    others = [
-        pltpu.make_async_copy(source, target, load_sem.at[NFLD + i])
-        for i, (source, target) in enumerate(surface + coupling)
+    top_rows = [(state.at[field * LEV], near_air.at[field, pl.ds(0, ROWS), :]) for field in range(2)]
+    pairs = top_rows + [
+        (sea_hbm, sea_int),
+        (place_hbm, place),
+        (weight_hbm, weight),
+        (mixing_hbm, mixing),
+        (remap_hbm, remap),
+        (offsets_hbm, offsets),
+        (live_hbm, live),
     ]
+    others = [pltpu.make_async_copy(*pair, load_sem.at[NFLD + i]) for i, pair in enumerate(pairs)]
+    for copy in others[:5]:
+        copy.start()
     for field in range(NFLD):
         load_of(field).start()
-    for copy in others:
+    for copy in others[5:]:
         copy.start()
 
     barrier = pltpu.get_barrier_semaphore()
@@ -115,36 +123,27 @@
         for strip in range(STRIPS):
             for device in (cell, right):
                 pl.semaphore_signal(barrier, inc=1, device_id=(strip, device), device_id_type=MESH)
-        pl.semaphore_wait(barrier, 2 + 2 * STRIPS)
 
     @pl.when(jnp.logical_not(is_ocean))
     def _():
         for device in (cell, left):
             pl.semaphore_signal(barrier, inc=1, device_id=(STRIPS, device), device_id_type=MESH)
-        pl.semaphore_wait(barrier, 4)
 
     def halo(step, field, side):
         levels = levels_of(field)
-        if step == 0:
-            source, low, high, target = state, 0, ROWS - RIM, first
+        source, low = ((state, 0), (second, TOP))[step]
+        if side == 0:
+            begin, land, device = low + ROWS - RIM, TOP - RIM, right
         else:
-            source, low, high, target = second, TOP, TOP + ROWS - RIM, second
-        if side == 0:
-            begin, land, device = high, TOP - RIM, right
-        else:
-            begin, land, device = low, TOP + ROWS, left
+            begin, land, device = low, 0, left
         return pltpu.make_async_remote_copy(
             src_ref=source.at[levels, pl.ds(begin, RIM), :],
-            dst_ref=target.at[levels, pl.ds(land, RIM), :],
+            dst_ref=rims.at[step, levels, pl.ds(land, RIM), :],
             send_sem=halo_send.at[step, side, field],
             recv_sem=halo_recv.at[step, side, field],
             device_id=(group, device),
             device_id_type=MESH,
         )
-
-    for field in range(NFLD):
-        for side in range(2):
-            halo(0, field, side).start()
 
     def sea_copy(strip, pair):
         return pltpu.make_async_remote_copy(
@@ -166,49 +165,68 @@
             device_id_type=MESH,
         )
 
-    for field in range(NFLD):
-        load_of(field).wait()
-    for copy in others:
+    for copy in others[:3]:
         copy.wait()
     sea_mask = sea_int[...].astype(jnp.float32)
 
     @pl.when(is_ocean)
     def _():
         for field in range(2):
-            sea_out[field] = first[field * LEV, TOP : TOP + ROWS, :] * sea_mask
+            sea_out[field] = near_air[field, 0:ROWS, :] * sea_mask
         sea_out[2] = sea_mask
+        pl.semaphore_wait(barrier, 2 + 2 * STRIPS)
         for strip in range(STRIPS):
             for pair in range(2):
                 sea_copy(strip, pair).start()
 
+    @pl.when(jnp.logical_not(is_ocean))
+    def _():
+        pl.semaphore_wait(barrier, 4)
+
+    for field in range(NFLD):
+        for side in range(2):
+            halo(0, field, side).start()
+    for copy in others[3:]:
+        copy.wait()
+
     lane8 = lax.broadcasted_iota(jnp.int32, (8, LANES), 1)
     row8 = lax.broadcasted_iota(jnp.int32, (8, LANES), 0)
     half = lane8 < LANES // 2
 
-    def advance(source, target, target_top, field, chunk):
-        rows = slice(chunk * 8, chunk * 8 + 8)
-        position = [place[k, rows, :] for k in range(3)]
+    upper = row8 < 4
+
+    def advance(source, target, target_top, field, chunks):
+        def take(load):
+            values = [load(8 * chunk) for chunk in chunks]
+            return values[0] if len(values) == 1 else jnp.where(upper, *values)
+
+        own_row = take(lambda row: row8 + (row + RIM))
+        position = [take(lambda row: place[k, row : row + 8, :]) for k in range(3)]
         index = [p & (LANES - 1) for p in position]
-        apart = [(p >> 7) - (row8 + (chunk * 8 + RIM)) for p in position]
-        part = [weight[k, rows, :] for k in range(3)]
+        apart = [(p >> 7) - own_row for p in position]
+        part = [take(lambda row: weight[k, row : row + 8, :]) for k in range(3)]
         centre = part[0] + part[1] + part[2]
-        scale = jnp.where(is_ocean, sea_int[rows, :].astype(jnp.float32), 1.0)
+        scale = jnp.where(is_ocean, take(lambda row: sea_int[row : row + 8, :]).astype(jnp.float32), 1.0)
         far_at = [apart[2] == g for g in (-2, -1, 1, 2)]
         here = [apart[k] == 0 for k in range(2)]
-        base = TOP + chunk * 8
         steps = LEV // BATCH
 
         def batch(t, carry):
             begin, below = carry
             level = t * BATCH
             at = field * LEV + level
-            x = [begin] + [source[at + b, pl.ds(base, 8), :] for b in range(1, BATCH + 1)]
-            before = [source[at + b, pl.ds(base - 1, 8), :] for b in range(BATCH)]
-            after = [source[at + b, pl.ds(base + 1, 8), :] for b in range(BATCH)]
+
+            def rows_at(b, shift):
+                return take(lambda row: source[at + b, pl.ds(TOP + row + shift, 8), :])
+
+            x = [begin] + [rows_at(b, 0) for b in range(1, BATCH)]
+            x.append(rows_at(jnp.minimum(BATCH, LEV - 1 - level), 0))
+            before = [rows_at(b, -1) for b in range(BATCH)]
+            after = [rows_at(b, 1) for b in range(BATCH)]
             mixed = []
             for b in range(BATCH):
-                before2 = source[at + b, pl.ds(base - 2, 8), :]
-                after2 = source[at + b, pl.ds(base + 2, 8), :]
+                before2 = rows_at(b, -2)
+                after2 = rows_at(b, 2)
                 value = lane_gather(x[b], index[2])
                 for chosen, row in zip(far_at, (before2, before[b], after[b], after2)):
                     value = jnp.where(chosen, lane_gather(row, index[2]), value)
@@ -219,26 +237,56 @@
                     value = jnp.where(here[k], lane_gather(x[b], index[k]), lane_gather(edge[b], index[k]))
                     mixed[b] = mixed[b] + part[k] * value
             for b in range(BATCH):
-                upward = mixing[level + b, rows, :] * (x[b + 1] - x[b])
+                upward = take(lambda row: mixing[level + b, row : row + 8, :]) * (x[b + 1] - x[b])
                 if b == BATCH - 1:
                     upward = jnp.where(t == steps - 1, 0.0, upward)
-                target[at + b, target_top + chunk * 8 : target_top + chunk * 8 + 8, :] = x[b] + scale * (
-                    mixed[b] + (upward - below)
-                )
+                result = x[b] + scale * (mixed[b] + (upward - below))
+                for i, chunk in enumerate(chunks):
+                    low, high = (0, 8) if len(chunks) == 1 else (4 * i, 4 * i + 4)
+                    row = target_top + 8 * chunk
+                    target[at + b, row + low : row + high, :] = result[low:high]
                 below = upward
             return x[BATCH], below
 
-        start = source[field * LEV, pl.ds(base, 8), :]
+        start = take(lambda row: source[field * LEV, pl.ds(TOP + row, 8), :])
         lax.fori_loop(0, steps, batch, (start, jnp.zeros((8, LANES), jnp.float32)))
 
-    def each_field(body):
-        lax.fori_loop(0, NFLD, lambda field, c: (body(field), c)[1], 0)
-
-    def inner_first(field):
-        for chunk in (1, 2):
-            advance(first, second, TOP, field, chunk)
-
-    each_field(inner_first)
+    last = ROWS // 8 - 1
+
+    def inner(source, target, target_top, field):
+        for chunks in ((1,), (2,), (last, 0)):
+            advance(source, target, target_top, field, chunks)
+
+    def outer(step, source, target, target_top, field):
+        for side in range(2):
+            halo(step, field, side).wait_recv()
+
+        def land(i, c):
+            for b in range(10):
+                at = field * LEV + i * 10 + b
+                source[at, TOP - RIM : TOP, :] = rims[step, at, TOP - RIM : TOP, :]
+                source[at, TOP + ROWS : TOP + ROWS + RIM, :] = rims[step, at, 0:RIM, :]
+            return c
+
+        lax.fori_loop(0, LEV // 10, land, 0)
+        advance(source, target, target_top, field, (0, last))
+
+    def first_section(turn, c):
+        @pl.when(turn < NFLD)
+        def _():
+            load_of(turn).wait()
+            inner(first, second, TOP, turn)
+
+        @pl.when(turn >= 1)
+        def _():
+            field = turn - 1
+            outer(0, first, second, TOP, field)
+            for side in range(2):
+                halo(1, field, side).start()
+
+        return c
+
+    lax.fori_loop(0, NFLD + 1, first_section, 0)
 
     lane1 = lax.broadcasted_iota(jnp.int32, (1, LANES), 1)
     lane3 = lax.broadcasted_iota(jnp.int32, (3, LANES), 1)
@@ -250,7 +298,6 @@
     def _():
         gap = [jnp.zeros((ROWS, LANES), jnp.float32) for _ in range(2)]
         for field in range(2):
-            near_air[field, 0:ROWS, :] = first[field * LEV, TOP : TOP + ROWS, :]
             near_air[field, ROWS:, :] = jnp.zeros((8, LANES), jnp.float32)
         for pair in range(2):
             sea_copy(0, pair).wait_recv()
@@ -319,19 +366,11 @@
                 for pair in range(2):
                     term_copy(strip, pair).start()
 
-    def outer_first(field):
-        for side, chunk in ((0, 0), (1, ROWS // 8 - 1)):
-            halo(0, field, side).wait_recv()
-            advance(first, second, TOP, field, chunk)
-            halo(1, field, 1 - side).start()
-
-    each_field(outer_first)
-
-    def inner_second(field):
-        for chunk in (1, 2):
-            advance(second, out, 0, field, chunk)
-
-    each_field(inner_second)
+    def inner_second(field, c):
+        inner(second, out, 0, field)
+        return c
+
+    lax.fori_loop(0, NFLD, inner_second, 0)
 
     @pl.when(is_ocean)
     def _():
@@ -346,12 +385,11 @@
         for field in range(2):
             flux[field, 0:ROWS, :] = -flux[field, 0:ROWS, :] * sea_mask
 
-    def outer_second(field):
-        for side, chunk in ((0, 0), (1, ROWS // 8 - 1)):
-            halo(1, field, side).wait_recv()
-            advance(second, out, 0, field, chunk)
-
-    each_field(outer_second)
+    def outer_second(field, c):
+        outer(1, second, out, 0, field)
+        return c
+
+    lax.fori_loop(0, NFLD, outer_second, 0)
 
     for step in range(2):
         for field in range(NFLD):
@@ -427,13 +465,14 @@
             pltpu.SMEM((2,), jnp.int32),
             pltpu.VMEM((levels + 2, 48, LANES), f32),
             pltpu.VMEM((levels + 2, 48, LANES), f32),
+            pltpu.VMEM((2, levels, 8, LANES), f32),
             pltpu.VMEM((LEV, ROWS, LANES), f32),
             pltpu.VMEM((3, ROWS, LANES), f32),
             pltpu.VMEM((2, 3, 16, LANES), f32),
             pltpu.VMEM((2, ROWS + 8, LANES), f32),
             pltpu.VMEM((2, 2, 16, LANES), f32),
             pltpu.VMEM((STRIPS, 2, 2, 16, LANES), f32),
-            dma((NFLD + 7,)),
+            dma((NFLD + 9,)),
             dma((2, 2, NFLD)),
             dma((2, 2, NFLD)),
             dma((STRIPS, 2)),

time: 50.3 us -> 46.7 us (0.928)
  the two profiles are of different devices: /device:TPU:1 before, /device:TPU:81 now
where the time goes in v4:
time: 46.7 us; the launch traced here: 46.5 us
  Pallas kernels  46.5 us (100%)
    pallas_call x1, Pallas kernels, per_device(): pl.pallas_call(functools.partial(window_kernel, n_cells), out_shape=(pltp...  44.4 us
    pallas_call x1, Pallas kernels, per_device(): pl.pallas_call(store_kernel, out_shape=jax.ShapeDtypeStruct((levels, ROWS...  2.13 us

profile of v4, /device:TPU:81, one launch (start us, length us, event | category | flops | bytes accessed | tf_op | source)
XLA Modules:
  0.0 46.5 jit_solution(14523829721577710645)
XLA Ops:
  0.0 44.4 %window.1 = (f32[270,32,128]{2,1,0:T(8,128)S(1)}, f32[2,40,128]{2,1,0:T(8,128)S(1)}) custom-call(f32[270,32,128]{2,1,0:T(8,128)} %bitcast.9, f32[90,32,128]{2,1,0:T(8,128)} %bitcast.10, f32[3,32,128]{2,1,0:T(8,128)} %bitcast.12, s32[3,32,128]{2,1,0:T(8,128)} %bitcast.13, s32[32,128]{1,0:T(8,128)} %bitcast.14, f32[2,256,256]{2,1,0:T(8,128)} %bitcast.11, ...), custom_call_target="tpu_custom_call" | custom-call | tf_op jit(solution)/shard_map/window/pallas_call | solution.py:454
  44.4 2.1 %store.1 = f32[270,32,128]{2,1,0:T(8,128)} custom-call(f32[270,32,128]{2,1,0:T(8,128)S(1)} %get-tuple-element.7.fields, f32[2,40,128]{2,1,0:T(8,128)S(1)} %get-tuple-element.8.forcing), custom_call_target="tpu_custom_call" | custom-call | tf_op jit(solution)/shard_map/store/pallas_call | solution.py:488

commit v5 on v4

--- a/solution.py
+++ b/solution.py
@@ -176,7 +176,7 @@
         sea_out[2] = sea_mask
         pl.semaphore_wait(barrier, 2 + 2 * STRIPS)
         for strip in range(STRIPS):
-            for pair in range(2):
+            for pair in range(1):
                 sea_copy(strip, pair).start()
 
     @pl.when(jnp.logical_not(is_ocean))
@@ -186,6 +186,11 @@
     for field in range(NFLD):
         for side in range(2):
             halo(0, field, side).start()
+    @pl.when(is_ocean)
+    def _():
+        for strip in range(STRIPS):
+            for pair in range(1, 2):
+                sea_copy(strip, pair).start()
     for copy in others[3:]:
         copy.wait()
 
@@ -271,31 +276,13 @@
         lax.fori_loop(0, LEV // 10, land, 0)
         advance(source, target, target_top, field, (0, last))
 
-    def first_section(turn, c):
-        @pl.when(turn < NFLD)
-        def _():
-            load_of(turn).wait()
-            inner(first, second, TOP, turn)
-
-        @pl.when(turn >= 1)
-        def _():
-            field = turn - 1
-            outer(0, first, second, TOP, field)
-            for side in range(2):
-                halo(1, field, side).start()
-
-        return c
-
-    lax.fori_loop(0, NFLD + 1, first_section, 0)
-
     lane1 = lax.broadcasted_iota(jnp.int32, (1, LANES), 1)
     lane3 = lax.broadcasted_iota(jnp.int32, (3, LANES), 1)
     lane2 = lax.broadcasted_iota(jnp.int32, (2, LANES), 1)
     row_of = lax.broadcasted_iota(jnp.int32, (ROWS, LANES), 0)
     slab_row = lax.broadcasted_iota(jnp.int32, (16, LANES), 0)
 
-    @pl.when(jnp.logical_not(is_ocean))
-    def _():
+    def couple():
         gap = [jnp.zeros((ROWS, LANES), jnp.float32) for _ in range(2)]
         for field in range(2):
             near_air[field, ROWS:, :] = jnp.zeros((8, LANES), jnp.float32)
@@ -366,11 +353,39 @@
                 for pair in range(2):
                     term_copy(strip, pair).start()
 
+    def first_section(turn, c):
+        @pl.when(turn < NFLD)
+        def _():
+            load_of(turn).wait()
+            inner(first, second, TOP, turn)
+
+        @pl.when(turn >= 1)
+        def _():
+            field = turn - 1
+            outer(0, first, second, TOP, field)
+            for side in range(2):
+                halo(1, field, side).start()
+
+        return c
+
+    lax.fori_loop(0, NFLD + 1, first_section, 0)
+
     def inner_second(field, c):
         inner(second, out, 0, field)
+
+        @pl.when(jnp.logical_not(is_ocean) & (field == 1))
+        def _():
+            couple()
+
         return c
 
     lax.fori_loop(0, NFLD, inner_second, 0)
+
+    def outer_second(field, c):
+        outer(1, second, out, 0, field)
+        return c
+
+    lax.fori_loop(0, NFLD, outer_second, 0)
 
     @pl.when(is_ocean)
     def _():
@@ -384,12 +399,6 @@
                     flux[field, at, :] = flux[field, at, :] + term_in[strip, pair, field, 0:SLAB, :]
         for field in range(2):
             flux[field, 0:ROWS, :] = -flux[field, 0:ROWS, :] * sea_mask
-
-    def outer_second(field, c):
-        outer(1, second, out, 0, field)
-        return c
-
-    lax.fori_loop(0, NFLD, outer_second, 0)
 
     for step in range(2):
         for field in range(NFLD):

time: 46.7 us -> 40.7 us (0.87)
  the two profiles are of different devices: /device:TPU:81 before, /device:TPU:86 now
where the time goes in v5:
time: 40.7 us; the launch traced here: 40.5 us
  Pallas kernels  40.5 us (100%)
    pallas_call x1, Pallas kernels, per_device(): pl.pallas_call(functools.partial(window_kernel, n_cells), out_shape=(pltp...  38.4 us
    pallas_call x1, Pallas kernels, per_device(): pl.pallas_call(store_kernel, out_shape=jax.ShapeDtypeStruct((levels, ROWS...  2.13 us

profile of v5, /device:TPU:86, one launch (start us, length us, event | category | flops | bytes accessed | tf_op | source)
XLA Modules:
  0.0 40.5 jit_solution(1174382017869917799)
XLA Ops:
  0.0 38.4 %window.1 = (f32[270,32,128]{2,1,0:T(8,128)S(1)}, f32[2,40,128]{2,1,0:T(8,128)S(1)}) custom-call(f32[270,32,128]{2,1,0:T(8,128)} %bitcast.9, f32[90,32,128]{2,1,0:T(8,128)} %bitcast.10, f32[3,32,128]{2,1,0:T(8,128)} %bitcast.12, s32[3,32,128]{2,1,0:T(8,128)} %bitcast.13, s32[32,128]{1,0:T(8,128)} %bitcast.14, f32[2,256,256]{2,1,0:T(8,128)} %bitcast.11, ...), custom_call_target="tpu_custom_call" | custom-call | tf_op jit(solution)/shard_map/window/pallas_call | solution.py:463
  38.4 2.1 %store.1 = f32[270,32,128]{2,1,0:T(8,128)} custom-call(f32[270,32,128]{2,1,0:T(8,128)S(1)} %get-tuple-element.7.fields, f32[2,40,128]{2,1,0:T(8,128)S(1)} %get-tuple-element.8.forcing), custom_call_target="tpu_custom_call" | custom-call | tf_op jit(solution)/shard_map/store/pallas_call | solution.py:497

commit v6 on v5

--- a/solution.py
+++ b/solution.py
@@ -13,7 +13,7 @@
 ROWS = 32
 TOP = 8
 RIM = 2
-BATCH = 45
+BATCH = 90
 SLAB = 12
 SLAB_STEP = 10
 STRIPS = 3
@@ -157,8 +157,8 @@
 
     def term_copy(strip, pair):
         return pltpu.make_async_remote_copy(
-            src_ref=term_out.at[pair],
-            dst_ref=term_in.at[strip, pair],
+            src_ref=term_out.at[pair, :, pl.ds(0, SLAB), :],
+            dst_ref=term_in.at[strip, pair, :, pl.ds(0, SLAB), :],
             send_sem=term_send.at[pair],
             recv_sem=term_recv.at[strip, pair],
             device_id=(STRIPS, (cell, left)[pair]),
@@ -298,14 +298,12 @@
                 lane3,
             )
             sea = [jnp.where(lane3 + i * LANES < rows_live, sea[i], 0.0) for i in range(2)]
-            moved = jnp.zeros((3, 2 * LANES), jnp.float32)
-            for i in range(2):
-                moved = moved + jnp.dot(
-                    sea[i],
-                    remap[pair, i * LANES : (i + 1) * LANES, :],
-                    precision=lax.Precision.HIGHEST,
-                    preferred_element_type=jnp.float32,
-                )
+            moved = jnp.dot(
+                jnp.concatenate(sea, axis=1),
+                remap[pair],
+                precision=lax.Precision.HIGHEST,
+                preferred_element_type=jnp.float32,
+            )
             for field in range(2):
                 air = window_pair(
                     [near_air[field, pl.ds(jnp.clip((col >> 7) + i, 0, ROWS), 1), :] for i in range(3)],
@@ -328,19 +326,17 @@
             back = window_pair(
                 [flux[:, jnp.clip((col >> 7) + i, 0, ROWS), :] for i in range(3)], col & (LANES - 1), lane2
             )
-            parts = []
-            for i in range(2):
-                block = remap[pair, i * LANES : (i + 1) * LANES, :]
-                term = jnp.zeros((2, LANES), jnp.float32)
-                for j in range(2):
-                    term = term + lax.dot_general(
-                        back[j],
-                        block[:, j * LANES : (j + 1) * LANES],
-                        (((1,), (1,)), ((), ())),
-                        precision=lax.Precision.HIGHEST,
-                        preferred_element_type=jnp.float32,
-                    )
-                parts.append(jnp.where(lane2 + i * LANES < rows_live, term, 0.0))
+            term = lax.dot_general(
+                jnp.concatenate(back, axis=1),
+                remap[pair],
+                (((1,), (1,)), ((), ())),
+                precision=lax.Precision.HIGHEST,
+                preferred_element_type=jnp.float32,
+            )
+            parts = [
+                jnp.where(lane2 + i * LANES < rows_live, term[:, i * LANES : (i + 1) * LANES], 0.0)
+                for i in range(2)
+            ]
             for field in range(2):
                 laid = placed(
                     [part[field : field + 1] for part in parts], row >> 7, row & (LANES - 1), lane1, slab_row
@@ -371,11 +367,13 @@
     lax.fori_loop(0, NFLD + 1, first_section, 0)
 
     def inner_second(field, c):
-        inner(second, out, 0, field)
-
-        @pl.when(jnp.logical_not(is_ocean) & (field == 1))
-        def _():
-            couple()
+        for order, chunks in enumerate(((1,), (2,), (last, 0))):
+            advance(second, out, 0, field, chunks)
+            if order == 0:
+
+                @pl.when(jnp.logical_not(is_ocean) & (field == 2))
+                def _():
+                    couple()
 
         return c
 

time: 40.7 us -> 39.9 us (0.980)
  the two profiles are of different devices: /device:TPU:86 before, /device:TPU:126 now
where the time goes in v6:
time: 39.9 us; the launch traced here: 39.8 us
  Pallas kernels  39.8 us (100%)
    pallas_call x1, Pallas kernels, per_device(): pl.pallas_call(functools.partial(window_kernel, n_cells), out_shape=(pltp...  37.7 us
    pallas_call x1, Pallas kernels, per_device(): pl.pallas_call(store_kernel, out_shape=jax.ShapeDtypeStruct((levels, ROWS...  2.13 us

profile of v6, /device:TPU:126, one launch (start us, length us, event | category | flops | bytes accessed | tf_op | source)
XLA Modules:
  0.0 39.8 jit_solution(3930689624371756452)
XLA Ops:
  0.0 37.7 %window.1 = (f32[270,32,128]{2,1,0:T(8,128)S(1)}, f32[2,40,128]{2,1,0:T(8,128)S(1)}) custom-call(f32[270,32,128]{2,1,0:T(8,128)} %bitcast.9, f32[90,32,128]{2,1,0:T(8,128)} %bitcast.10, f32[3,32,128]{2,1,0:T(8,128)} %bitcast.12, s32[3,32,128]{2,1,0:T(8,128)} %bitcast.13, s32[32,128]{1,0:T(8,128)} %bitcast.14, f32[2,256,256]{2,1,0:T(8,128)} %bitcast.11, ...), custom_call_target="tpu_custom_call" | custom-call | tf_op jit(solution)/shard_map/window/pallas_call | solution.py:461
  37.7 2.1 %store.1 = f32[270,32,128]{2,1,0:T(8,128)} custom-call(f32[270,32,128]{2,1,0:T(8,128)S(1)} %get-tuple-element.7.fields, f32[2,40,128]{2,1,0:T(8,128)S(1)} %get-tuple-element.8.forcing), custom_call_target="tpu_custom_call" | custom-call | tf_op jit(solution)/shard_map/store/pallas_call | solution.py:495

commit v7 on v6

--- a/solution.py
+++ b/solution.py
@@ -107,11 +107,11 @@
         (live_hbm, live),
     ]
     others = [pltpu.make_async_copy(*pair, load_sem.at[NFLD + i]) for i, pair in enumerate(pairs)]
-    for copy in others[:5]:
+    for copy in others[:6]:
         copy.start()
     for field in range(NFLD):
         load_of(field).start()
-    for copy in others[5:]:
+    for copy in others[6:]:
         copy.start()
 
     barrier = pltpu.get_barrier_semaphore()
@@ -191,7 +191,7 @@
         for strip in range(STRIPS):
             for pair in range(1, 2):
                 sea_copy(strip, pair).start()
-    for copy in others[3:]:
+    for copy in others[3:6]:
         copy.wait()
 
     lane8 = lax.broadcasted_iota(jnp.int32, (8, LANES), 1)
@@ -365,6 +365,8 @@
         return c
 
     lax.fori_loop(0, NFLD + 1, first_section, 0)
+    for copy in others[6:]:
+        copy.wait()
 
     def inner_second(field, c):
         for order, chunks in enumerate(((1,), (2,), (last, 0))):

time: 39.9 us -> 40 us (level)
  no operation moved by 1% of the time
where the time goes in v7:
time: 40 us; the launch traced here: 39.8 us
  Pallas kernels  39.8 us (99%)
    pallas_call x1, Pallas kernels, per_device(): pl.pallas_call(functools.partial(window_kernel, n_cells), out_shape=(pltp...  37.7 us
    pallas_call x1, Pallas kernels, per_device(): pl.pallas_call(store_kernel, out_shape=jax.ShapeDtypeStruct((levels, ROWS...  2.13 us

profile of v7, /device:TPU:126, one launch (start us, length us, event | category | flops | bytes accessed | tf_op | source)
XLA Modules:
  0.0 39.8 jit_solution(5205001097599753231)
XLA Ops:
  0.0 37.7 %window.1 = (f32[270,32,128]{2,1,0:T(8,128)S(1)}, f32[2,40,128]{2,1,0:T(8,128)S(1)}) custom-call(f32[270,32,128]{2,1,0:T(8,128)} %bitcast.9, f32[90,32,128]{2,1,0:T(8,128)} %bitcast.10, f32[3,32,128]{2,1,0:T(8,128)} %bitcast.12, s32[3,32,128]{2,1,0:T(8,128)} %bitcast.13, s32[32,128]{1,0:T(8,128)} %bitcast.14, f32[2,256,256]{2,1,0:T(8,128)} %bitcast.11, ...), custom_call_target="tpu_custom_call" | custom-call | tf_op jit(solution)/shard_map/window/pallas_call | solution.py:463
  37.7 2.1 %store.1 = f32[270,32,128]{2,1,0:T(8,128)} custom-call(f32[270,32,128]{2,1,0:T(8,128)S(1)} %get-tuple-element.7.fields, f32[2,40,128]{2,1,0:T(8,128)S(1)} %get-tuple-element.8.forcing), custom_call_target="tpu_custom_call" | custom-call | tf_op jit(solution)/shard_map/store/pallas_call | solution.py:497
